TPU v7x, 32 devices: a whole 2x2x4 slice. The times are simulated.
32 devices in a mesh: groups: 2 (over y), store: 4 (over x, core), tensor: 4 (over z).
Axes of the slice: x: 2, y: 2, z: 4, core: 2. Of those that a mesh axis runs over, the one named last changes fastest.
Arguments:
- tokens: bfloat16 [112, 8192], P(('groups', 'tensor'), 'store'), parts along dimension 0, may hold values from -6 to 6
- adapter_ids: int32 [112], P('groups'), parts along dimension 0, may hold values from 0 to 31
- store_slot: int32 [32], replicated, may hold values from 0 to 31, each once
- w_gate: bfloat16 [8192, 14336], P('store', 'tensor'), may hold values from -0.0625 to 0.0625
- w_up: bfloat16 [8192, 14336], P('store', 'tensor'), may hold values from -0.0625 to 0.0625
- w_down: bfloat16 [14336, 8192], P('tensor', 'store'), may hold values from -0.046875 to 0.046875
- a_gate: bfloat16 [32, 16, 8192], P('tensor', None, 'store'), may hold values from -0.0625 to 0.0625
- b_gate: bfloat16 [32, 16, 14336], P('store', None, 'tensor'), may hold values from -1.5 to 1.5
- a_up: bfloat16 [32, 16, 8192], P('tensor', None, 'store'), may hold values from -0.0625 to 0.0625
- b_up: bfloat16 [32, 16, 14336], P('store', None, 'tensor'), may hold values from -1.5 to 1.5
- a_down: bfloat16 [32, 16, 14336], P('store', None, 'tensor'), may hold values from -0.046875 to 0.046875
- b_down: bfloat16 [32, 16, 8192], P('tensor', None, 'store'), may hold values from -1.5 to 1.5
Outputs:
- mixed: bfloat16 [112, 8192], P(('groups', 'tensor'), 'store'), parts along dimension 0
There are 2 independent parts, one for each index of `groups`. A program takes and returns all parts, laid end to end along the dimension named above; an argument that names none is the same for every part. Nothing has to cross between parts.
Inputs may be any that keep to these rules, and one draw needn't show every extreme that they name: `adapter_ids`: adapter of each request, an index into store_slot. `store_slot`: every store place is used by exactly one adapter.
All inputs are finite; a program needn't handle non-finite values.
Results may differ from a plain program's by a relative error of at most 0.0062.
Values may be sent and summed in bfloat16 or wider, within the bound.
A program may use at most 128 MiB of HBM per device.

v0:
```python
import jax
import jax.numpy as jnp
from jax import lax
from jax.sharding import PartitionSpec as P


def local_hot(place, first, number):
    columns = first + jnp.arange(number, dtype=jnp.int32)
    return (place[:, None] == columns[None, :]).astype(jnp.bfloat16)


def pick_rank(products, place_hot):
    shaped = products.reshape(products.shape[0], place_hot.shape[1], -1)
    return jnp.sum(shaped * place_hot.astype(jnp.float32)[:, :, None], axis=1)


def spread_rank(low_rank, place_hot):
    spread = place_hot[:, :, None] * low_rank[:, None, :]
    return spread.reshape(low_rank.shape[0], -1)


def project_rank(values, factors):
    flat = factors.reshape(-1, factors.shape[2])
    return jnp.einsum("rd,kd->rk", values, flat, preferred_element_type=jnp.float32)


def shards(
    tokens,
    adapter_ids,
    store_slot,
    w_gate,
    w_up,
    w_down,
    a_gate,
    b_gate,
    a_up,
    b_up,
    a_down,
    b_down,
):
    adapters = store_slot.shape[0]
    id_hot = adapter_ids[:, None] == jnp.arange(adapters, dtype=jnp.int32)[None, :]
    place = jnp.sum(jnp.where(id_hot, store_slot[None, :], 0), axis=1)
    tensor_block = a_gate.shape[0]
    store_block = b_gate.shape[0]
    tensor_hot = local_hot(place, lax.axis_index("tensor") * tensor_block, tensor_block)
    store_hot = local_hot(place, lax.axis_index("store") * store_block, store_block)
    gathered = lax.all_gather(tokens, "tensor", axis=0, tiled=True)
    gate_part = pick_rank(project_rank(gathered, a_gate), tensor_hot)
    up_part = pick_rank(project_rank(gathered, a_up), tensor_hot)
    gate_low, up_low = lax.psum((gate_part, up_part), ("store", "tensor"))
    gate_low = gate_low.astype(jnp.bfloat16)
    up_low = up_low.astype(jnp.bfloat16)
    gate_terms = jnp.dot(gathered, w_gate, preferred_element_type=jnp.float32)
    gate_terms = gate_terms + jnp.dot(
        spread_rank(gate_low, store_hot),
        b_gate.reshape(-1, b_gate.shape[2]),
        preferred_element_type=jnp.float32,
    )
    up_terms = jnp.dot(gathered, w_up, preferred_element_type=jnp.float32)
    up_terms = up_terms + jnp.dot(
        spread_rank(up_low, store_hot),
        b_up.reshape(-1, b_up.shape[2]),
        preferred_element_type=jnp.float32,
    )
    gate_share, up_share = (
        lax.psum_scatter(gate_terms, "store", scatter_dimension=0, tiled=True),
        lax.psum_scatter(up_terms, "store", scatter_dimension=0, tiled=True),
    )
    hidden_share = (jax.nn.silu(gate_share) * up_share).astype(jnp.bfloat16)
    hidden = lax.all_gather(hidden_share, "store", axis=0, tiled=True)
    down_part = pick_rank(project_rank(hidden, a_down), store_hot)
    down_low = lax.psum(down_part, ("store", "tensor")).astype(jnp.bfloat16)
    out_terms = jnp.dot(hidden, w_down, preferred_element_type=jnp.float32)
    out_terms = out_terms + jnp.dot(
        spread_rank(down_low, tensor_hot),
        b_down.reshape(-1, b_down.shape[2]),
        preferred_element_type=jnp.float32,
    )
    return lax.psum_scatter(out_terms, "tensor", scatter_dimension=0, tiled=True).astype(
        jnp.bfloat16
    )


def solution(mesh):
    return jax.shard_map(
        shards,
        mesh=mesh,
        in_specs=(
            P(("groups", "tensor"), "store"),
            P("groups"),
            P(),
            P("store", "tensor"),
            P("store", "tensor"),
            P("tensor", "store"),
            P("tensor", None, "store"),
            P("store", None, "tensor"),
            P("tensor", None, "store"),
            P("store", None, "tensor"),
            P("store", None, "tensor"),
            P("tensor", None, "store"),
        ),
        out_specs=P(("groups", "tensor"), "store"),
        check_vma=False,
    )
```

profile of v0, /device:TPU:0, one launch (start us, length us, event | category | flops | bytes accessed | tf_op | source)
XLA Modules:
  0.0 189.0 jit_solution(17684157911135304668)
XLA Ops:
  0.0 16.0 %all-gather = bf16[4,14,2048]{2,1,0:T(8,128)(2,1)S(1)} all-gather(bf16[1,14,2048]{2,1,0:T(8,128)(2,1)} %bitcast.35), channel_id=1, replica_groups=mesh['groups'=2,'store'=4,'tensor'=4] {'tensor'}, dimensions={0}, use_global_device_ids=true | all-gather | bytes 286720 | tf_op jit(solution)/shard_map/all_gather | solution.py:48
  16.0 0.1 reshape.143
  16.0 0.1 reshape.140
  16.1 0.8 select_reduce_fusion
  16.9 0.1 compare_convert_fusion
  17.0 1.3 fusion.5
  18.3 1.3 fusion.6
  19.6 59.9 %all-reduce.6 = (bf16[56,16]{0,1:T(8,128)(2,1)S(1)}, bf16[56,16]{0,1:T(8,128)(2,1)S(1)}) all-reduce(f32[56,16]{0,1:T(8,128)S(1)} %fusion.6, f32[56,16]{0,1:T(8,128)S(1)} %fusion.5), channel_id=1, replica_groups=mesh['groups'=2,'store'=4,'tensor'=4] {'store','tensor'}, use_global_device_ids=true, to_apply=%region_5.6 | all-reduce | flops 1792 | bytes 10752 | tf_op jit(solution)/shard_map/psum | solution.py:51
  79.5 0.3 convolution_bitcast_fusion.1
  79.8 1.6 convolution_bitcast_fusion
  81.5 8.2 %convolution_add_fusion.1 = f32[56,3584]{1,0:T(8,128)S(1)} fusion(f32[56,3584]{1,0:T(8,128)S(1)} %convolution_bitcast_fusion.1, bf16[56,2048]{1,0:T(8,128)(2,1)S(1)} %reshape.140, bf16[2048,3584]{1,0:T(8,128)(2,1)} %param.15), kind=kOutput, calls=%fused_computation.1 | convolution fusion | flops 822284288 | bytes 16515072 | tf_op jit(solution)/shard_map/dot_general | solution.py:54
  89.7 2.6 %convolution_add_fusion = f32[56,3584]{1,0:T(8,128)S(1)} fusion(f32[56,3584]{1,0:T(8,128)S(1)} %convolution_bitcast_fusion, bf16[56,2048]{1,0:T(8,128)(2,1)S(1)} %reshape.140, bf16[2048,3584]{1,0:T(8,128)(2,1)S(1)} %copy-done.1), kind=kOutput, calls=%fused_computation | convolution fusion | flops 822284288 | bytes 16515072 | tf_op jit(solution)/shard_map/dot_general | solution.py:60
  92.3 20.0 %fusion.20 = (f32[16,3584]{1,0:T(8,128)S(1)}, f32[16,3584]{1,0:T(8,128)S(1)}) fusion(f32[56,3584]{1,0:T(8,128)S(1)} %convolution_add_fusion, f32[56,3584]{1,0:T(8,128)S(1)} %convolution_add_fusion.1), kind=kCustom, calls=%all-reduce-scatter.3 | all-reduce-scatter fusion | flops 458753 | bytes 2064896
  112.3 1.4 collective-permute-start
  113.8 3.4 %collective-permute-start.1 = (f32[6,3584]{1,0:T(8,128)S(1)}, f32[6,3584]{1,0:T(8,128)S(1)}, u32[]{:S(2)}, u32[]{:S(2)}) collective-permute-start(f32[6,3584]{1,0:T(8,128)S(1)} %slice.1), channel_id=1, source_target_pairs={{0,4},{4,8},{8,12},{1,5},{5,9},{9,13},{2,6},{6,10},{10,14},{3,7},{... | collective-permute-start | bytes 258056
  117.1 0.6 dynamic-slice.8
  118.4 0.3 concatenate
  118.7 0.3 concatenate.1
  119.0 0.1 fusion.8
  119.1 7.8 %all-gather.1 = bf16[4,14,3584]{2,1,0:T(8,128)(2,1)S(1)} all-gather(bf16[1,14,3584]{2,1,0:T(8,128)(2,1)S(1)} %fusion.8), channel_id=1, replica_groups=mesh['groups'=2,'store'=4,'tensor'=4] {'store'}, dimensions={0}, use_global_device_ids=true | all-gather | bytes 501760 | tf_op jit(solution)/shard_map/all_gather | solution.py:71
  127.0 0.1 reshape.142
  127.1 0.1 reshape.146
  127.2 1.6 fusion.4
  128.8 30.4 %psum.23 = bf16[56,16]{0,1:T(8,128)(2,1)S(1)} all-reduce(f32[56,16]{0,1:T(8,128)S(1)} %fusion.4), channel_id=1, replica_groups=mesh['groups'=2,'store'=4,'tensor'=4] {'store','tensor'}, use_global_device_ids=true, to_apply=%region_8.9 | all-reduce | flops 896 | bytes 5376 | tf_op jit(solution)/shard_map/psum | solution.py:73
  159.2 7.7 %fusion.21 = f32[56,2048]{1,0:T(8,128)S(1)} fusion(bf16[56,3584]{1,0:T(8,128)(2,1)S(1)} %reshape.142, bf16[3584,2048]{1,0:T(8,128)(2,1)} %param.17), kind=kOutput, calls=%fused_computation.33 | convolution fusion | flops 822083584 | bytes 15540224 | tf_op jit(solution)/shard_map/dot_general | solution.py:74
  167.0 0.3 fusion.3
  167.2 17.3 %fusion.2 = f32[16,2048]{1,0:T(8,128)S(1)} fusion(f32[56,2048]{1,0:T(8,128)S(1)} %fusion.3), kind=kCustom, calls=%all-reduce-scatter.2 | all-reduce-scatter fusion | flops 131073 | bytes 590336
  184.6 2.0 %collective-permute-start.2 = (bf16[6,2048]{1,0:T(8,128)(2,1)S(1)}, bf16[6,2048]{1,0:T(8,128)(2,1)S(1)}, u32[]{:S(2)}, u32[]{:S(2)}) collective-permute-start(bf16[6,2048]{1,0:T(8,128)(2,1)S(1)} %slice.2), channel_id=1, source_target_pairs={{0,1},{1,2},{2,3},{4,5},{5,6},{6,7},{8,9},{9,10},{10,11},{12,13},{... | collective-permute-start | bytes 73736
  186.6 0.6 dynamic-slice.16
  187.8 0.3 collective-permute-done.2
  188.2 0.2 concatenate.2
  188.4 0.7 dynamic-slice_convert_fusion
  (16 shorter events, 0.1 us)
Async XLA Ops:
  0.0 79.5 %copy-start = (bf16[8,16,3584]{2,1,0:T(8,128)(2,1)S(1)}, bf16[8,16,3584]{2,1,0:T(8,128)(2,1)}, u32[]{:S(2)}) copy-start(bf16[8,16,3584]{2,1,0:T(8,128)(2,1)} %param.19) | copy-start | bytes 2752516
  79.5 10.2 %copy-start.1 = (bf16[2048,3584]{1,0:T(8,128)(2,1)S(1)}, bf16[2048,3584]{1,0:T(8,128)(2,1)}, u32[]{:S(2)}) copy-start(bf16[2048,3584]{1,0:T(8,128)(2,1)} %param.16) | copy-start | bytes 44040196
  89.7 27.4 %copy-start.4 = (u32[32]{0:T(128)S(1)}, u32[32]{0:T(128)}, u32[]{:S(2)}) copy-start(u32[32]{0:T(128)} %constant.19) | copy-start | bytes 388
  112.3 54.7 %copy-start.2 = (bf16[8,16,2048]{2,1,0:T(8,128)(2,1)S(1)}, bf16[8,16,2048]{2,1,0:T(8,128)(2,1)}, u32[]{:S(2)}) copy-start(bf16[8,16,2048]{2,1,0:T(8,128)(2,1)} %param.23) | copy-start | bytes 1572868
  112.3 6.1 %collective-permute-start = (f32[6,3584]{1,0:T(8,128)S(1)}, f32[6,3584]{1,0:T(8,128)S(1)}, u32[]{:S(2)}, u32[]{:S(2)}) collective-permute-start(f32[6,3584]{1,0:T(8,128)S(1)} %slice), channel_id=1, source_target_pairs={{0,4},{4,8},{8,12},{1,5},{5,9},{9,13},{2,6},{6,10},{10,14},{3,7},{... | collective-permute-start | bytes 258056
  113.8 4.9 %collective-permute-start.1 = (f32[6,3584]{1,0:T(8,128)S(1)}, f32[6,3584]{1,0:T(8,128)S(1)}, u32[]{:S(2)}, u32[]{:S(2)}) collective-permute-start(f32[6,3584]{1,0:T(8,128)S(1)} %slice.1), channel_id=1, source_target_pairs={{0,4},{4,8},{8,12},{1,5},{5,9},{9,13},{2,6},{6,10},{10,14},{3,7},{... | collective-permute-start | bytes 258056
  119.0 67.6 %copy-start.3 = (u32[32]{0:T(128)S(1)}, u32[32]{0:T(128)}, u32[]{:S(2)}) copy-start(u32[32]{0:T(128)} %constant.27) | copy-start | bytes 388
  184.6 3.6 %collective-permute-start.2 = (bf16[6,2048]{1,0:T(8,128)(2,1)S(1)}, bf16[6,2048]{1,0:T(8,128)(2,1)S(1)}, u32[]{:S(2)}, u32[]{:S(2)}) collective-permute-start(bf16[6,2048]{1,0:T(8,128)(2,1)S(1)} %slice.2), channel_id=1, source_target_pairs={{0,1},{1,2},{2,3},{4,5},{5,6},{6,7},{8,9},{9,10},{10,11},{12,13},{... | collective-permute-start | bytes 73736
where the time goes:
time: 189 us
  blocking collectives  151 us (80%)
  matrix products  25 us (13%)
  starting transfers between devices  6.78 us (4%)
  local copies, waits for them, and re-layouts  3.06 us (2%)
    psum x1, blocking collectives, shards(): gate_low, up_low = lax.psum((gate_part, up_part), ('store', 'tensor'))  59.9 us
    unnamed x2, blocking collectives  37.3 us
    psum x1, blocking collectives, shards(): down_low = lax.psum(down_part, ('store', 'tensor')).astype(jnp.bfloat16)  30.4 us
    all_gather x1, blocking collectives, shards(): gathered = lax.all_gather(tokens, 'tensor', axis=0, tiled=True)  16 us
    dot_general x1, matrix products, shards(): gate_terms = jnp.dot(gathered, w_gate, preferred_element_type=jnp.float32)  8.22 us
    all_gather x1, blocking collectives, shards(): hidden = lax.all_gather(hidden_share, 'store', axis=0, tiled=True)  7.83 us
    dot_general x1, matrix products, shards(): out_terms = jnp.dot(hidden, w_down, preferred_element_type=jnp.float32)  7.74 us
    unnamed x3, starting transfers between devices  6.78 us
  transfers between devices with their start and end apart: 3, of which 1 were waited for; matrix products, arithmetic and copies ran while one was open for 1% of the time, Pallas kernels for 0%

commit v1 on v0

v1 whole, which is shorter than its diff:
```python
import functools

import jax
import jax.numpy as jnp
from jax import lax
from jax.experimental import pallas as pl
from jax.experimental.pallas import tpu as pltpu
from jax.sharding import PartitionSpec as P

MESH = pl.DeviceIdType.MESH
BF = jnp.bfloat16
F32 = jnp.float32
PAD = 16
CHUNKS = 7
OUT_CHUNKS = 4
LAG_B, LAG_H, LAG_F, LAG_D = 1, 2, 3, 4


def nt_dot(a, b):
    return lax.dot_general(a, b, (((1,), (1,)), ((), ())), preferred_element_type=F32)


def kernel(
    S,
    T,
    rank,
    tok_ref,
    ids_ref,
    slot_ref,
    wg_hbm,
    wu_hbm,
    wd_hbm,
    ag_hbm,
    bg_hbm,
    au_hbm,
    bu_hbm,
    ad_hbm,
    bd_hbm,
    out_ref,
    wg,
    wu,
    wd,
    ag,
    bg,
    au,
    bu,
    ad,
    bd,
    tok,
    hot_t,
    hot_s,
    acc,
    send_a,
    recv_a,
    send_b,
    recv_b,
    hid,
    lacc,
    oacc,
    osend,
    orecv,
    low_mine,
    low_store,
    low_sum,
    low_tensor,
    dlow_mine,
    dlow_store,
    dlow_sum,
    dlow_tensor,
    w_sem,
    f_sem,
    tok_ss,
    tok_rs,
    ls_ss,
    ls_rs,
    lt_ss,
    lt_rs,
    ds_ss,
    ds_rs,
    dt_ss,
    dt_rs,
    a_ss,
    a_rs,
    b_ss,
    b_rs,
    h_ss,
    h_rs,
    g_ss,
    g_rs,
    k_ss,
    k_rs,
    o_ss,
    o_rs,
):
    X = S // 2
    s = lax.axis_index("store")
    t = lax.axis_index("tensor")
    x, c = s // 2, s % 2
    sib = x * 2 + (1 - c)
    n = tok_ref.shape[0]
    rows = T * PAD
    depth = tok.shape[2]
    nc = wg.shape[2]
    lanes = ag.shape[0]
    groups = lanes // rank
    on = oacc.shape[2]

    def weight(hbm, buf, j, sem):
        return pltpu.make_async_copy(hbm.at[:, pl.ds(j * nc, nc)], buf.at[j], sem)

    cg = [weight(wg_hbm, wg, j, w_sem.at[0, j]) for j in range(CHUNKS)]
    cu = [weight(wu_hbm, wu, j, w_sem.at[1, j]) for j in range(CHUNKS)]
    cd = [
        pltpu.make_async_copy(wd_hbm.at[pl.ds(j * nc, nc), :], wd.at[j], w_sem.at[2, j])
        for j in range(CHUNKS)
    ]
    cag = pltpu.make_async_copy(ag_hbm, ag, f_sem.at[0])
    cau = pltpu.make_async_copy(au_hbm, au, f_sem.at[1])
    cbg = pltpu.make_async_copy(bg_hbm, bg, f_sem.at[2])
    cbu = pltpu.make_async_copy(bu_hbm, bu, f_sem.at[3])
    cad = pltpu.make_async_copy(ad_hbm, ad, f_sem.at[4])
    cbd = pltpu.make_async_copy(bd_hbm, bd, f_sem.at[5])

    barrier = pltpu.get_barrier_semaphore()
    for d in range(1, S):
        pl.semaphore_signal(
            barrier, inc=1, device_id={"store": (s + d) % S}, device_id_type=MESH
        )
    for d in range(1, T):
        pl.semaphore_signal(
            barrier, inc=1, device_id={"tensor": (t + d) % T}, device_id_type=MESH
        )
    cag.start()
    cau.start()
    for j in range(CHUNKS):
        cg[j].start()
        cu[j].start()
        if j == 1:
            cbg.start()
            cbu.start()
    cad.start()
    for j in range(CHUNKS):
        cd[j].start()
    cbd.start()

    tok[t] = jnp.zeros((PAD, depth), BF)
    tok[t, 0:n, :] = tok_ref[...]
    pl.semaphore_wait(barrier, S + T - 2)

    def remote(src, dst, ss, rs, axis, index):
        return pltpu.make_async_remote_copy(
            src_ref=src,
            dst_ref=dst,
            send_sem=ss,
            recv_sem=rs,
            device_id={axis: index},
            device_id_type=MESH,
        )

    sent = []

    def go(copy):
        copy.start()
        sent.append(copy)
        return copy

    tcopies = [
        go(remote(tok.at[t], tok.at[t], tok_ss.at[d - 1], tok_rs.at[d - 1], "tensor", (t + d) % T))
        for d in range(1, T)
    ]

    lane_group = lax.broadcasted_iota(jnp.int32, (1, lanes), 1) // rank
    hot_t[...] = jnp.zeros_like(hot_t)
    hot_s[...] = jnp.zeros_like(hot_s)

    def mark(r, carry):
        place = slot_ref[ids_ref[r]]
        row = (r // n) * PAD + r % n
        hot_t[pl.ds(row, 1), :] = jnp.where(lane_group == place - t * groups, 1.0, 0.0)
        hot_s[pl.ds(row, 1), :] = jnp.where(lane_group == place - s * groups, 1.0, 0.0)
        return carry

    lax.fori_loop(0, n * T, mark, 0)

    fold = (
        lax.broadcasted_iota(jnp.int32, (lanes, lanes), 0) % rank
        == lax.broadcasted_iota(jnp.int32, (lanes, lanes), 1) % rank
    )
    own_group = (
        lax.broadcasted_iota(jnp.int32, (rows, lanes), 0) % groups
        == lax.broadcasted_iota(jnp.int32, (rows, lanes), 1) // rank
    )

    def pack(part):
        spread = jnp.dot(
            part, fold.astype(F32), precision=lax.Precision.HIGHEST, preferred_element_type=F32
        )
        spread = jnp.where(own_group, spread, 0.0)
        return jnp.sum(spread.reshape(rows // groups, groups, lanes), axis=1)

    def unpack(packed, hot):
        spread = jnp.broadcast_to(packed[:, None, :], (rows // groups, groups, lanes))
        spread = jnp.where(own_group, spread.reshape(rows, lanes), 0.0).astype(BF)
        low = jnp.dot(spread, fold.astype(F32).astype(BF), preferred_element_type=F32)
        return (low * hot[...]).astype(BF)

    def exchange(mine, slots, ss, rs, axis, me, size):
        return [
            go(remote(mine, slots.at[d - 1], ss.at[d - 1], rs.at[d - 1], axis, (me + d) % size))
            for d in range(1, size)
        ]

    def gather_sum(mine, slots, copies):
        total = mine[...]
        for d, copy in enumerate(copies):
            copy.wait_recv()
            total = total + slots[d]
        return total

    for copy in tcopies:
        copy.wait_recv()
    tokens = tok[...].reshape(rows, depth)

    cag.wait()
    cau.wait()
    low_mine[0] = pack(nt_dot(tokens, ag[...]) * hot_t[...])
    low_mine[1] = pack(nt_dot(tokens, au[...]) * hot_t[...])
    ls = exchange(low_mine, low_store, ls_ss, ls_rs, "store", s, S)

    q = rows // S

    def main(j):
        cg[j].wait()
        g = jnp.dot(tok[...].reshape(rows, depth), wg[j], preferred_element_type=F32)
        acc[j, :, :, 0:nc] = g.reshape(S, q, nc)
        cu[j].wait()
        u = jnp.dot(tok[...].reshape(rows, depth), wu[j], preferred_element_type=F32)
        acc[j, :, :, nc:] = u.reshape(S, q, nc)

    acopies, bcopies, hcopies, gcopies, kcopies = {}, {}, {}, {}, {}

    def finish(j, spread_g, spread_u):
        cols = pl.ds(j * nc, nc)
        acc[j, :, :, 0:nc] += jnp.dot(
            spread_g, bg[:, cols], preferred_element_type=F32
        ).reshape(S, q, nc)
        acc[j, :, :, nc:] += jnp.dot(
            spread_u, bu[:, cols], preferred_element_type=F32
        ).reshape(S, q, nc)
        for k in range(X):
            send_a[j, k] = acc[j, 2 * k + (1 - c)].astype(BF)
        acopies[j] = go(remote(send_a.at[j], recv_a.at[j], a_ss.at[j], a_rs.at[j], "store", sib))

    def stage_b(j):
        acopies[j].wait_recv()
        bcopies[j] = []
        for d in range(1, X):
            xo = (x + d) % X
            send_b[j, d - 1] = (acc[j, 2 * xo + c] + recv_a[j, xo].astype(F32)).astype(BF)
            bcopies[j].append(
                go(
                    remote(
                        send_b.at[j, d - 1],
                        recv_b.at[j, d - 1],
                        b_ss.at[j, d - 1],
                        b_rs.at[j, d - 1],
                        "store",
                        xo * 2 + c,
                    )
                )
            )

    def stage_h(j):
        total = acc[j, s] + recv_a[j, x].astype(F32)
        for d in range(1, X):
            bcopies[j][d - 1].wait_recv()
            total = total + recv_b[j, d - 1].astype(F32)
        gate, up = total[:, 0:nc], total[:, nc:]
        hid[j, s] = (gate / (1.0 + jnp.exp(-gate)) * up).astype(BF)
        gcopies[j] = [
            go(
                remote(
                    hid.at[j, s],
                    hid.at[j, s],
                    g_ss.at[j, d - 1],
                    g_rs.at[j, d - 1],
                    "store",
                    ((x + d) % X) * 2 + c,
                )
            )
            for d in range(1, X)
        ]
        hcopies[j] = go(
            remote(hid.at[j, s], hid.at[j, s], h_ss.at[j], h_rs.at[j], "store", sib)
        )

    def stage_f(j):
        kcopies[j] = []
        for d in range(1, X):
            gcopies[j][d - 1].wait_recv()
            origin = ((x - d + X) % X) * 2 + c
            kcopies[j].append(
                go(
                    remote(
                        hid.at[j, origin],
                        hid.at[j, origin],
                        k_ss.at[j, d - 1],
                        k_rs.at[j, d - 1],
                        "store",
                        sib,
                    )
                )
            )

    def stage_d(j):
        hcopies[j].wait_recv()
        for copy in kcopies[j]:
            copy.wait_recv()
        h = hid[j].reshape(rows, nc)
        if j == 0:
            cad.wait()
        low = nt_dot(h, ad[:, pl.ds(j * nc, nc)])
        lacc[...] = low if j == 0 else lacc[...] + low
        last = j == CHUNKS - 1
        copies = None
        if last:
            dlow_mine[...] = pack(lacc[...] * hot_s[...])
            copies = exchange(dlow_mine, dlow_store, ds_ss, ds_rs, "store", s, S)
        cd[j].wait()
        half = OUT_CHUNKS // 2
        for k in range(OUT_CHUNKS):
            if last and k == half:
                dlow_sum[...] = gather_sum(dlow_mine, dlow_store, copies)
                copies = exchange(dlow_sum, dlow_tensor, dt_ss, dt_rs, "tensor", t, T)
            o = jnp.dot(
                hid[j].reshape(rows, nc), wd[j, :, k * on : (k + 1) * on], preferred_element_type=F32
            )
            oacc[k] = o if j == 0 else oacc[k] + o
        return copies

    main(0)
    low_sum[...] = gather_sum(low_mine, low_store, ls)
    lt = exchange(low_sum, low_tensor, lt_ss, lt_rs, "tensor", t, T)
    main(1)
    main(2)
    low = gather_sum(low_sum, low_tensor, lt)
    spread_g = unpack(low[0], hot_s)
    spread_u = unpack(low[1], hot_s)
    cbg.wait()
    cbu.wait()

    copies = None
    done_h = 0
    for i in range(CHUNKS + LAG_D):
        if 3 <= i < CHUNKS:
            main(i)
        if i < CHUNKS:
            finish(i, spread_g, spread_u)
        if 0 <= i - LAG_B < CHUNKS:
            stage_b(i - LAG_B)
        if 0 <= i - LAG_H < CHUNKS:
            stage_h(i - LAG_H)
        if 0 <= i - LAG_F < CHUNKS:
            stage_f(i - LAG_F)
        if 0 <= i - LAG_D < CHUNKS:
            copies = stage_d(i - LAG_D)

    dlow = gather_sum(dlow_sum, dlow_tensor, copies)
    spread_d = unpack(dlow, hot_t)
    cbd.wait()
    ocopies = []
    own = []
    for k in range(OUT_CHUNKS):
        o = oacc[k] + jnp.dot(
            spread_d, bd[:, k * on : (k + 1) * on], preferred_element_type=F32
        )
        oacc[k] = o
        osend[k] = o.reshape(T, PAD, on).astype(BF)
        ocopies.append(
            [
                go(
                    remote(
                        osend.at[k, (t + d) % T],
                        orecv.at[k, d - 1],
                        o_ss.at[k, d - 1],
                        o_rs.at[k, d - 1],
                        "tensor",
                        (t + d) % T,
                    )
                )
                for d in range(1, T)
            ]
        )
    for k in range(OUT_CHUNKS):
        total = oacc[k, pl.ds(pl.multiple_of(t * PAD, PAD), PAD), :]
        for d in range(1, T):
            ocopies[k][d - 1].wait_recv()
            total = total + orecv[k, d - 1].astype(F32)
        out_ref[:, k * on : (k + 1) * on] = total[0:n].astype(BF)
    for copy in sent:
        copy.wait_send()


def solution(mesh):
    S, T = mesh.shape["store"], mesh.shape["tensor"]
    X = S // 2

    def shards(tokens, ids, slot, wg, wu, wd, ag, bg, au, bu, ad, bd):
        n, depth = tokens.shape
        ff = wg.shape[1]
        cols = wd.shape[1]
        rank = ag.shape[1]
        flat = lambda v: v.reshape(-1, v.shape[2])
        ag, bg, au, bu, ad, bd = map(flat, (ag, bg, au, bu, ad, bd))
        lanes = ag.shape[0]
        nc = ff // CHUNKS
        on = cols // OUT_CHUNKS
        rows = T * PAD
        q = rows // S
        groups = lanes // rank
        packed = (rows // groups, lanes)
        vm = pltpu.VMEM
        dma = lambda *shape: pltpu.SemaphoreType.DMA(shape)
        pair = lambda *shape: [dma(*shape), dma(*shape)]
        scratch = [
            vm((CHUNKS, depth, nc), BF),
            vm((CHUNKS, depth, nc), BF),
            vm((CHUNKS, nc, cols), BF),
            vm(ag.shape, BF),
            vm(bg.shape, BF),
            vm(au.shape, BF),
            vm(bu.shape, BF),
            vm(ad.shape, BF),
            vm(bd.shape, BF),
            vm((T, PAD, depth), BF),
            vm((rows, lanes), F32),
            vm((rows, lanes), F32),
            vm((CHUNKS, S, q, 2 * nc), F32),
            vm((CHUNKS, X, q, 2 * nc), BF),
            vm((CHUNKS, X, q, 2 * nc), BF),
            vm((CHUNKS, X - 1, q, 2 * nc), BF),
            vm((CHUNKS, X - 1, q, 2 * nc), BF),
            vm((CHUNKS, S, q, nc), BF),
            vm((rows, lanes), F32),
            vm((OUT_CHUNKS, rows, on), F32),
            vm((OUT_CHUNKS, T, PAD, on), BF),
            vm((OUT_CHUNKS, T - 1, PAD, on), BF),
            vm((2,) + packed, F32),
            vm((S - 1, 2) + packed, F32),
            vm((2,) + packed, F32),
            vm((T - 1, 2) + packed, F32),
            vm(packed, F32),
            vm((S - 1,) + packed, F32),
            vm(packed, F32),
            vm((T - 1,) + packed, F32),
            dma(3, CHUNKS),
            dma(6),
            *pair(T - 1),
            *pair(S - 1),
            *pair(T - 1),
            *pair(S - 1),
            *pair(T - 1),
            *pair(CHUNKS),
            *pair(CHUNKS, X - 1),
            *pair(CHUNKS),
            *pair(CHUNKS, X - 1),
            *pair(CHUNKS, X - 1),
            *pair(OUT_CHUNKS, T - 1),
        ]
        smem = pl.BlockSpec(memory_space=pltpu.SMEM)
        vmem = pl.BlockSpec(memory_space=pltpu.VMEM)
        hbm = pl.BlockSpec(memory_space=pl.ANY)
        return pl.pallas_call(
            functools.partial(kernel, S, T, rank),
            out_shape=jax.ShapeDtypeStruct((n, cols), BF),
            in_specs=[vmem, smem, smem] + [hbm] * 9,
            out_specs=vmem,
            scratch_shapes=scratch,
            compiler_params=pltpu.CompilerParams(
                collective_id=0, has_side_effects=True, vmem_limit_bytes=60 * 1024 * 1024
            ),
        )(tokens, ids, slot, wg, wu, wd, ag, bg, au, bu, ad, bd)

    return jax.shard_map(
        shards,
        mesh=mesh,
        in_specs=(
            P(("groups", "tensor"), "store"),
            P("groups"),
            P(),
            P("store", "tensor"),
            P("store", "tensor"),
            P("tensor", "store"),
            P("tensor", None, "store"),
            P("store", None, "tensor"),
            P("tensor", None, "store"),
            P("store", None, "tensor"),
            P("store", None, "tensor"),
            P("tensor", None, "store"),
        ),
        out_specs=P(("groups", "tensor"), "store"),
        check_vma=False,
    )
```

time: 189 us -> 59.1 us (0.31)
  blocking collectives: 151 us -> 0 us
  Pallas kernels: 0 us -> 57.4 us
  matrix products: 25 us -> 0 us
  starting transfers between devices: 6.78 us -> 0 us
    psum x2 -> x0, blocking collectives: 90.3 us -> none  [the longest x1 59.9 us: shards(): gate_low, up_low = lax.psum((gate_part, up_part), ('store', 'tensor'))]
    pallas_call x0 -> x1, Pallas kernels: none -> 57.4 us  [shards(): pl.pallas_call(functools.partial(kernel, S, T, rank), out_shape=jax.Shape...]
    unnamed x2 -> x0, blocking collectives: 37.3 us -> none
    dot_general x9 -> x0, matrix products: 25 us -> none  [the longest x1 8.22 us: shards(): gate_terms = jnp.dot(gathered, w_gate, preferred_element_type=jnp.float32)]
    all_gather x2 -> x0, blocking collectives: 23.8 us -> none  [the longest x1 16 us: shards(): gathered = lax.all_gather(tokens, 'tensor', axis=0, tiled=True)]
    unnamed x3 -> x0, starting transfers between devices: 6.78 us -> none
  transfers between devices with their start and end apart: 3 -> 0, of which waited for: 1 -> 0; matrix products, arithmetic and copies ran while one was open for 1% -> 0% of each run, Pallas kernels for 0% -> 0%
where the time goes in v1:
time: 59.1 us; the launch traced here: 58.9 us
  Pallas kernels  57.4 us (97%)
  local copies, waits for them, and re-layouts  1.47 us (2%)
    pallas_call x1, Pallas kernels, shards(): pl.pallas_call(functools.partial(kernel, S, T, rank), out_shape=jax.Shape...  57.4 us
    unnamed x1, local copies, waits for them, and re-layouts  1.47 us

profile of v1, /device:TPU:0, one launch (start us, length us, event | category | flops | bytes accessed | tf_op | source)
XLA Modules:
  0.0 58.9 jit_solution(2755873234993187184)
XLA Ops:
  0.0 57.4 %shard_map.118 = bf16[14,2048]{1,0:T(8,128)(2,1)} custom-call(bf16[14,2048]{1,0:T(8,128)(2,1)} %tok_ref.1, s32[56]{0:T(128)} %ids_ref.1, s32[32]{0:T(128)} %slot_ref.1, bf16[2048,3584]{1,0:T(8,128)(2,1)} %wg_hbm.1, bf16[2048,3584]{1,0:T(8,128)(2,1)} %wu_hbm.1, bf16[3584,2048]{1,0:T(8,128)(2,1)} %wd_hbm.1, bf16[128,2048]{1,0:T(8,128)(2,1)} %bitcast.9, ...), custom_call_target="tpu_custom_call" | custom-call | tf_op jit(solution)/shard_map/pallas_call | solution.py:473
  57.4 1.5 %copy.14 = bf16[14,2048]{1,0:T(8,128)(2,1)} copy(bf16[14,2048]{1,0:T(8,128)(2,1)} %shard_map.118) | data formatting | bytes 114688

commit v2 on v1

--- a/solution.py
+++ b/solution.py
@@ -13,7 +13,27 @@
 PAD = 16
 CHUNKS = 7
 OUT_CHUNKS = 4
-LAG_B, LAG_H, LAG_F, LAG_D = 1, 2, 3, 4
+SPLIT = 2
+EARLY = 3
+AHEAD = 5
+HOLD = 2
+WINDOW = 6
+FIRST = 0
+LAG_B, LAG_H, LAG_F, LAG_D = 1, 3, 5, 6
+
+
+def plan():
+    order = []
+    for i in range(CHUNKS + LAG_D):
+        steps = [("m", i)] if AHEAD <= i < CHUNKS else []
+        steps += [("a", i), ("b", i - LAG_B), ("h", i - LAG_H), ("f", i - LAG_F), ("l", i - LAG_D)]
+        if i - LAG_D < CHUNKS - HOLD:
+            steps += [("d", i - LAG_D)]
+        order += [(kind, j) for kind, j in steps if 0 <= j < CHUNKS]
+    return order
+
+
+ORDER = plan()
 
 
 def nt_dot(a, b):
@@ -99,7 +119,7 @@
     sib = x * 2 + (1 - c)
     n = tok_ref.shape[0]
     rows = T * PAD
-    depth = tok.shape[2]
+    kd = tok.shape[3]
     nc = wg.shape[2]
     lanes = ag.shape[0]
     groups = lanes // rank
@@ -130,21 +150,27 @@
         pl.semaphore_signal(
             barrier, inc=1, device_id={"tensor": (t + d) % T}, device_id_type=MESH
         )
-    cag.start()
-    cau.start()
+    line = [cag, cau]
     for j in range(CHUNKS):
-        cg[j].start()
-        cu[j].start()
+        line += [cg[j], cu[j]]
         if j == 1:
-            cbg.start()
-            cbu.start()
-    cad.start()
-    for j in range(CHUNKS):
-        cd[j].start()
-    cbd.start()
-
-    tok[t] = jnp.zeros((PAD, depth), BF)
-    tok[t, 0:n, :] = tok_ref[...]
+            line += [cbg, cbu]
+    line += [cad] + cd + [cbd]
+    waited = []
+    for copy in line[:WINDOW]:
+        copy.start()
+
+    def need(copy):
+        while not any(copy is w for w in waited):
+            k = len(waited)
+            line[k].wait()
+            waited.append(line[k])
+            if k + WINDOW < len(line):
+                line[k + WINDOW].start()
+
+    for h in range(SPLIT):
+        tok[h, t] = jnp.zeros((PAD, kd), BF)
+        tok[h, t, 0:n, :] = tok_ref[:, h * kd : (h + 1) * kd]
     pl.semaphore_wait(barrier, S + T - 2)
 
     def remote(src, dst, ss, rs, axis, index):
@@ -165,8 +191,20 @@
         return copy
 
     tcopies = [
-        go(remote(tok.at[t], tok.at[t], tok_ss.at[d - 1], tok_rs.at[d - 1], "tensor", (t + d) % T))
-        for d in range(1, T)
+        [
+            go(
+                remote(
+                    tok.at[h, t],
+                    tok.at[h, t],
+                    tok_ss.at[h, d - 1],
+                    tok_rs.at[h, d - 1],
+                    "tensor",
+                    (t + d) % T,
+                )
+            )
+            for d in range(1, T)
+        ]
+        for h in range(SPLIT)
     ]
 
     lane_group = lax.broadcasted_iota(jnp.int32, (1, lanes), 1) // rank
@@ -217,25 +255,43 @@
             total = total + slots[d]
         return total
 
-    for copy in tcopies:
-        copy.wait_recv()
-    tokens = tok[...].reshape(rows, depth)
-
-    cag.wait()
-    cau.wait()
-    low_mine[0] = pack(nt_dot(tokens, ag[...]) * hot_t[...])
-    low_mine[1] = pack(nt_dot(tokens, au[...]) * hot_t[...])
+    q = rows // S
+
+    def half(h):
+        return tok[h].reshape(rows, kd)
+
+    def main_part(j, h):
+        ks = slice(h * kd, (h + 1) * kd)
+        for first, buf, copies in ((0, wg, cg), (nc, wu, cu)):
+            need(copies[j])
+            v = jnp.dot(half(h), buf[j, ks, :], preferred_element_type=F32).reshape(S, q, nc)
+            if h > 0:
+                v = v + acc[j, :, :, first : first + nc]
+            acc[j, :, :, first : first + nc] = v
+
+    def main(j):
+        need(cu[j])
+        for first, buf in ((0, wg), (nc, wu)):
+            v = 0.0
+            for h in range(SPLIT):
+                v = v + jnp.dot(
+                    half(h), buf[j, h * kd : (h + 1) * kd, :], preferred_element_type=F32
+                )
+            acc[j, :, :, first : first + nc] = v.reshape(S, q, nc)
+
+    lows = [0.0, 0.0]
+    for h in range(SPLIT):
+        need(cu[h + FIRST])
+        for copy in tcopies[h]:
+            copy.wait_recv()
+        for k, buf in enumerate((ag, au)):
+            lows[k] = lows[k] + nt_dot(half(h), buf[:, h * kd : (h + 1) * kd])
+        if h < SPLIT - 1:
+            for j in range(EARLY):
+                main_part(j, h)
+    low_mine[0] = pack(lows[0] * hot_t[...])
+    low_mine[1] = pack(lows[1] * hot_t[...])
     ls = exchange(low_mine, low_store, ls_ss, ls_rs, "store", s, S)
-
-    q = rows // S
-
-    def main(j):
-        cg[j].wait()
-        g = jnp.dot(tok[...].reshape(rows, depth), wg[j], preferred_element_type=F32)
-        acc[j, :, :, 0:nc] = g.reshape(S, q, nc)
-        cu[j].wait()
-        u = jnp.dot(tok[...].reshape(rows, depth), wu[j], preferred_element_type=F32)
-        acc[j, :, :, nc:] = u.reshape(S, q, nc)
 
     acopies, bcopies, hcopies, gcopies, kcopies = {}, {}, {}, {}, {}
 
@@ -312,62 +368,61 @@
                 )
             )
 
-    def stage_d(j):
+    def stage_l(j):
         hcopies[j].wait_recv()
         for copy in kcopies[j]:
             copy.wait_recv()
-        h = hid[j].reshape(rows, nc)
         if j == 0:
-            cad.wait()
-        low = nt_dot(h, ad[:, pl.ds(j * nc, nc)])
+            need(cad)
+        low = nt_dot(hid[j].reshape(rows, nc), ad[:, pl.ds(j * nc, nc)])
         lacc[...] = low if j == 0 else lacc[...] + low
-        last = j == CHUNKS - 1
-        copies = None
-        if last:
+        if j == CHUNKS - 1:
             dlow_mine[...] = pack(lacc[...] * hot_s[...])
-            copies = exchange(dlow_mine, dlow_store, ds_ss, ds_rs, "store", s, S)
-        cd[j].wait()
-        half = OUT_CHUNKS // 2
+            return exchange(dlow_mine, dlow_store, ds_ss, ds_rs, "store", s, S)
+
+    def stage_d(j):
+        need(cd[j])
         for k in range(OUT_CHUNKS):
-            if last and k == half:
-                dlow_sum[...] = gather_sum(dlow_mine, dlow_store, copies)
-                copies = exchange(dlow_sum, dlow_tensor, dt_ss, dt_rs, "tensor", t, T)
             o = jnp.dot(
                 hid[j].reshape(rows, nc), wd[j, :, k * on : (k + 1) * on], preferred_element_type=F32
             )
             oacc[k] = o if j == 0 else oacc[k] + o
-        return copies
-
-    main(0)
+
+    for j in range(EARLY):
+        main_part(j, SPLIT - 1)
     low_sum[...] = gather_sum(low_mine, low_store, ls)
     lt = exchange(low_sum, low_tensor, lt_ss, lt_rs, "tensor", t, T)
-    main(1)
-    main(2)
+    for j in range(EARLY, AHEAD):
+        main(j)
     low = gather_sum(low_sum, low_tensor, lt)
     spread_g = unpack(low[0], hot_s)
     spread_u = unpack(low[1], hot_s)
-    cbg.wait()
-    cbu.wait()
+    need(cbu)
 
     copies = None
-    done_h = 0
-    for i in range(CHUNKS + LAG_D):
-        if 3 <= i < CHUNKS:
-            main(i)
-        if i < CHUNKS:
-            finish(i, spread_g, spread_u)
-        if 0 <= i - LAG_B < CHUNKS:
-            stage_b(i - LAG_B)
-        if 0 <= i - LAG_H < CHUNKS:
-            stage_h(i - LAG_H)
-        if 0 <= i - LAG_F < CHUNKS:
-            stage_f(i - LAG_F)
-        if 0 <= i - LAG_D < CHUNKS:
-            copies = stage_d(i - LAG_D)
-
+    for kind, j in ORDER:
+        if kind == "m":
+            main(j)
+        elif kind == "a":
+            finish(j, spread_g, spread_u)
+        elif kind == "b":
+            stage_b(j)
+        elif kind == "h":
+            stage_h(j)
+        elif kind == "f":
+            stage_f(j)
+        elif kind == "l":
+            copies = stage_l(j) or copies
+        elif kind == "d":
+            stage_d(j)
+
+    dlow_sum[...] = gather_sum(dlow_mine, dlow_store, copies)
+    copies = exchange(dlow_sum, dlow_tensor, dt_ss, dt_rs, "tensor", t, T)
+    for j in range(CHUNKS - HOLD, CHUNKS):
+        stage_d(j)
     dlow = gather_sum(dlow_sum, dlow_tensor, copies)
     spread_d = unpack(dlow, hot_t)
-    cbd.wait()
+    need(cbd)
     ocopies = []
     own = []
     for k in range(OUT_CHUNKS):
@@ -432,7 +487,7 @@
             vm(bu.shape, BF),
             vm(ad.shape, BF),
             vm(bd.shape, BF),
-            vm((T, PAD, depth), BF),
+            vm((SPLIT, T, PAD, depth // SPLIT), BF),
             vm((rows, lanes), F32),
             vm((rows, lanes), F32),
             vm((CHUNKS, S, q, 2 * nc), F32),
@@ -455,7 +510,7 @@
             vm((T - 1,) + packed, F32),
             dma(3, CHUNKS),
             dma(6),
-            *pair(T - 1),
+            *pair(SPLIT, T - 1),
             *pair(S - 1),
             *pair(T - 1),
             *pair(S - 1),

time: 59.1 us -> 51.5 us (0.87)
  Pallas kernels: 57.4 us -> 49.9 us
    pallas_call x1, Pallas kernels: 57.4 us -> 49.9 us  [shards(): pl.pallas_call(functools.partial(kernel, S, T, rank), out_shape=jax.Shape...]
where the time goes in v2:
time: 51.5 us; the launch traced here: 51.3 us
  Pallas kernels  49.9 us (97%)
  local copies, waits for them, and re-layouts  1.47 us (3%)
    pallas_call x1, Pallas kernels, shards(): pl.pallas_call(functools.partial(kernel, S, T, rank), out_shape=jax.Shape...  49.9 us
    unnamed x1, local copies, waits for them, and re-layouts  1.47 us

profile of v2, /device:TPU:0, one launch (start us, length us, event | category | flops | bytes accessed | tf_op | source)
XLA Modules:
  0.0 51.3 jit_solution(12460807122544808738)
XLA Ops:
  0.0 49.9 %shard_map.118 = bf16[14,2048]{1,0:T(8,128)(2,1)} custom-call(bf16[14,2048]{1,0:T(8,128)(2,1)} %tok_ref.1, s32[56]{0:T(128)} %ids_ref.1, s32[32]{0:T(128)} %slot_ref.1, bf16[2048,3584]{1,0:T(8,128)(2,1)} %wg_hbm.1, bf16[2048,3584]{1,0:T(8,128)(2,1)} %wu_hbm.1, bf16[3584,2048]{1,0:T(8,128)(2,1)} %wd_hbm.1, bf16[128,2048]{1,0:T(8,128)(2,1)} %bitcast.9, ...), custom_call_target="tpu_custom_call" | custom-call | tf_op jit(solution)/shard_map/pallas_call | solution.py:528
  49.9 1.5 %copy.14 = bf16[14,2048]{1,0:T(8,128)(2,1)} copy(bf16[14,2048]{1,0:T(8,128)(2,1)} %shard_map.118) | data formatting | bytes 114688

commit v3 on v2

--- a/solution.py
+++ b/solution.py
@@ -14,19 +14,20 @@
 CHUNKS = 7
 OUT_CHUNKS = 4
 SPLIT = 2
-EARLY = 3
-AHEAD = 5
+EARLY = 1
+MID = 2
+AHEAD = 4
 HOLD = 2
 WINDOW = 6
 FIRST = 0
-LAG_B, LAG_H, LAG_F, LAG_D = 1, 3, 5, 6
+LAG_B, LAG_H, LAG_D = 1, 3, 5
 
 
 def plan():
     order = []
     for i in range(CHUNKS + LAG_D):
         steps = [("m", i)] if AHEAD <= i < CHUNKS else []
-        steps += [("a", i), ("b", i - LAG_B), ("h", i - LAG_H), ("f", i - LAG_F), ("l", i - LAG_D)]
+        steps += [("a", i), ("b", i - LAG_B), ("h", i - LAG_H), ("l", i - LAG_D)]
         if i - LAG_D < CHUNKS - HOLD:
             steps += [("d", i - LAG_D)]
         order += [(kind, j) for kind, j in steps if 0 <= j < CHUNKS]
@@ -333,44 +334,30 @@
             total = total + recv_b[j, d - 1].astype(F32)
         gate, up = total[:, 0:nc], total[:, nc:]
         hid[j, s] = (gate / (1.0 + jnp.exp(-gate)) * up).astype(BF)
-        gcopies[j] = [
-            go(
-                remote(
-                    hid.at[j, s],
-                    hid.at[j, s],
-                    g_ss.at[j, d - 1],
-                    g_rs.at[j, d - 1],
-                    "store",
-                    ((x + d) % X) * 2 + c,
+        def peers(ss, rs, core):
+            return [
+                go(
+                    remote(
+                        hid.at[j, s],
+                        hid.at[j, s],
+                        ss.at[j, d - 1],
+                        rs.at[j, d - 1],
+                        "store",
+                        ((x + d) % X) * 2 + core,
+                    )
                 )
-            )
-            for d in range(1, X)
-        ]
+                for d in range(1, X)
+            ]
+
+        gcopies[j] = peers(g_ss, g_rs, c)
+        kcopies[j] = peers(k_ss, k_rs, 1 - c)
         hcopies[j] = go(
             remote(hid.at[j, s], hid.at[j, s], h_ss.at[j], h_rs.at[j], "store", sib)
         )
 
-    def stage_f(j):
-        kcopies[j] = []
-        for d in range(1, X):
-            gcopies[j][d - 1].wait_recv()
-            origin = ((x - d + X) % X) * 2 + c
-            kcopies[j].append(
-                go(
-                    remote(
-                        hid.at[j, origin],
-                        hid.at[j, origin],
-                        k_ss.at[j, d - 1],
-                        k_rs.at[j, d - 1],
-                        "store",
-                        sib,
-                    )
-                )
-            )
-
     def stage_l(j):
         hcopies[j].wait_recv()
-        for copy in kcopies[j]:
+        for copy in gcopies[j] + kcopies[j]:
             copy.wait_recv()
         if j == 0:
             need(cad)
@@ -390,9 +377,11 @@
 
     for j in range(EARLY):
         main_part(j, SPLIT - 1)
+    for j in range(EARLY, MID):
+        main(j)
     low_sum[...] = gather_sum(low_mine, low_store, ls)
     lt = exchange(low_sum, low_tensor, lt_ss, lt_rs, "tensor", t, T)
-    for j in range(EARLY, AHEAD):
+    for j in range(MID, AHEAD):
         main(j)
     low = gather_sum(low_sum, low_tensor, lt)
     spread_g = unpack(low[0], hot_s)
@@ -409,8 +398,6 @@
             stage_b(j)
         elif kind == "h":
             stage_h(j)
-        elif kind == "f":
-            stage_f(j)
         elif kind == "l":
             copies = stage_l(j) or copies
         elif kind == "d":

time: 51.5 us -> 52.6 us (1.021)
  Pallas kernels: 49.9 us -> 50.9 us
    pallas_call x1, Pallas kernels: 49.9 us -> 50.9 us  [shards(): pl.pallas_call(functools.partial(kernel, S, T, rank), out_shape=jax.Shape...]
where the time goes in v3:
time: 52.6 us; the launch traced here: 52.4 us
  Pallas kernels  50.9 us (97%)
  local copies, waits for them, and re-layouts  1.47 us (3%)
    pallas_call x1, Pallas kernels, shards(): pl.pallas_call(functools.partial(kernel, S, T, rank), out_shape=jax.Shape...  50.9 us
    unnamed x1, local copies, waits for them, and re-layouts  1.47 us

profile of v3, /device:TPU:0, one launch (start us, length us, event | category | flops | bytes accessed | tf_op | source)
XLA Modules:
  0.0 52.4 jit_solution(16191181249507408328)
XLA Ops:
  0.0 50.9 %shard_map.118 = bf16[14,2048]{1,0:T(8,128)(2,1)} custom-call(bf16[14,2048]{1,0:T(8,128)(2,1)} %tok_ref.1, s32[56]{0:T(128)} %ids_ref.1, s32[32]{0:T(128)} %slot_ref.1, bf16[2048,3584]{1,0:T(8,128)(2,1)} %wg_hbm.1, bf16[2048,3584]{1,0:T(8,128)(2,1)} %wu_hbm.1, bf16[3584,2048]{1,0:T(8,128)(2,1)} %wd_hbm.1, bf16[128,2048]{1,0:T(8,128)(2,1)} %bitcast.9, ...), custom_call_target="tpu_custom_call" | custom-call | tf_op jit(solution)/shard_map/pallas_call | solution.py:515
  50.9 1.5 %copy.14 = bf16[14,2048]{1,0:T(8,128)(2,1)} copy(bf16[14,2048]{1,0:T(8,128)(2,1)} %shard_map.118) | data formatting | bytes 114688
